TPU v7x, 32 devices: a whole 2x2x4 slice. The times are simulated.
32 devices in a mesh: dp: 8 (over z, x), expert: 4 (over y, core).
Axes of the slice: x: 2, y: 2, z: 4, core: 2. Of those that a mesh axis runs over, the one named last changes fastest.
Arguments:
- tokens: bfloat16 [64, 197, 768], P(('dp', 'expert')), may hold values from -6 to 6
- route_ids: int32 [64, 197, 2], P(('dp', 'expert')), may hold values from 0 to 3, all different within a row; in each aligned block of 394 rows (0 to 393, 394 to 787, ..., all dimensions but the last counted through in order) at most 295 rows name the same one
- cotangent: bfloat16 [64, 197, 768], P(('dp', 'expert')), may hold values from -6 to 6
- norm1_gain: float32 [768], replicated, may hold values from 0.5 to 1.5
- norm1_shift: float32 [768], replicated, may hold values from -1 to 1
- qkv_weight: bfloat16 [768, 2304], replicated, may hold values from -0.21875 to 0.21875
- qv_bias: float32 [2, 768], replicated, may hold values from -1 to 1
- out_weight: bfloat16 [768, 768], replicated, may hold values from -1.5 to 1.5
- out_bias: float32 [768], replicated, may hold values from -1 to 1
- norm2_gain: float32 [768], replicated, may hold values from 0.5 to 1.5
- norm2_shift: float32 [768], replicated, may hold values from -1 to 1
- router_weight: bfloat16 [768, 4], replicated, may hold values from -0.15625 to 0.15625
- expert_in: bfloat16 [4, 768, 3072], P('expert'), may hold values from -0.21875 to 0.21875
- expert_in_bias: float32 [4, 3072], P('expert'), may hold values from -1 to 1
- expert_out: bfloat16 [4, 3072, 768], P('expert'), may hold values from -0.4375 to 0.4375
- expert_out_bias: float32 [4, 768], P('expert'), may hold values from -2 to 2
Outputs:
- output: bfloat16 [64, 197, 768], P(('dp', 'expert'))
- grad_tokens: float32 [64, 197, 768], P(('dp', 'expert'))
- grad_norm1_gain: float32 [768], replicated
- grad_norm1_shift: float32 [768], replicated
- grad_qkv_weight: float32 [768, 2304], replicated
- grad_qv_bias: float32 [2, 768], replicated
- grad_out_weight: float32 [768, 768], replicated
- grad_out_bias: float32 [768], replicated
- grad_norm2_gain: float32 [768], replicated
- grad_norm2_shift: float32 [768], replicated
- grad_router_weight: float32 [768, 4], replicated
- grad_expert_in: float32 [4, 768, 3072], P('expert', None, 'dp')
- grad_expert_in_bias: float32 [4, 3072], P('expert', 'dp')
- grad_expert_out: float32 [4, 3072, 768], P('expert', 'dp')
- grad_expert_out_bias: float32 [4, 768], P('expert', 'dp')
Inputs may be any that keep to these rules, and one draw needn't show every extreme that they name: `route_ids`: each token names two different experts. Among the tokens of one device no expert is named more than 295 times, and in every draw some expert is named exactly 295 times by the tokens of some device.
All inputs are finite; a program needn't handle non-finite values.
Results may differ from a plain program's by a relative error of at most 0.02.
Values may be sent and summed in bfloat16 or wider, within the bound.
A program may use at most 192 MiB of HBM per device.

v0:
```python
import math

import jax
import jax.numpy as jnp
from jax import lax
from jax.sharding import PartitionSpec as P

D = 768
HEADS = 12
HEAD = 64


epsilon = 1e-06


def normalize(values):
    mean_row = jnp.mean(values, axis=-1, keepdims=True)
    centred = values - mean_row
    variance = jnp.mean(centred * centred, axis=-1, keepdims=True)
    inv_dev = lax.rsqrt(variance + epsilon)
    return (centred * inv_dev, inv_dev)


def norm_back(grad_in, normed, inv_dev, gain):
    gain_grad = jnp.sum(grad_in * normed, axis=0)
    shift_grad = jnp.sum(grad_in, axis=0)
    scaled = grad_in * gain
    first_mean = jnp.mean(scaled, axis=-1, keepdims=True)
    second_mean = jnp.mean(scaled * normed, axis=-1, keepdims=True)
    return (gain_grad, shift_grad, inv_dev * (scaled - first_mean - normed * second_mean))


def local(
    tokens,
    route_ids,
    cotangent,
    norm1_gain,
    norm1_shift,
    qkv_weight,
    qv_bias,
    out_weight,
    out_bias,
    norm2_gain,
    norm2_shift,
    router_weight,
    expert_in,
    expert_in_bias,
    expert_out,
    expert_out_bias,
):
    images = tokens.shape[0]
    length = tokens.shape[1]
    row_count = images * length
    experts = lax.axis_size("expert")
    capacity = 3 * row_count // experts
    inv_root = 1.0 / math.sqrt(HEAD)
    lowtype = jnp.bfloat16
    inputs = tokens.astype(jnp.float32).reshape(row_count, D)
    normed1, inv_dev1 = normalize(inputs)
    hidden1 = (normed1 * norm1_gain + norm1_shift).astype(lowtype)
    bias_row = jnp.concatenate([qv_bias[0], jnp.zeros((D,), jnp.float32), qv_bias[1]])
    qkv_rows = (jnp.dot(hidden1, qkv_weight, preferred_element_type=jnp.float32) + bias_row).astype(
        lowtype
    )
    qkv_heads = qkv_rows.reshape(images, length, 3, HEADS, HEAD)
    query_rows = qkv_heads[:, :, 0]
    key_rows = qkv_heads[:, :, 1]
    value_rows = qkv_heads[:, :, 2]
    scores = (
        jnp.einsum("bqhd,bkhd->bhqk", query_rows, key_rows, preferred_element_type=jnp.float32)
        * inv_root
    )
    top_score = jnp.max(scores, axis=-1, keepdims=True)
    exp_scores = jnp.exp(scores - top_score)
    exp_total = jnp.sum(exp_scores, axis=-1, keepdims=True)
    attn_probs = exp_scores / exp_total
    log_total = top_score + jnp.log(exp_total)
    mixed_rows = jnp.einsum(
        "bhqk,bkhd->bqhd",
        attn_probs.astype(lowtype),
        value_rows,
        preferred_element_type=jnp.float32,
    )
    mixed_rows = mixed_rows.reshape(row_count, D).astype(lowtype)
    attn_out = jnp.dot(mixed_rows, out_weight, preferred_element_type=jnp.float32) + out_bias
    resid = inputs + attn_out
    normed2, inv_dev2 = normalize(resid)
    hidden2 = (normed2 * norm2_gain + norm2_shift).astype(lowtype)
    logits = jnp.dot(hidden2, router_weight, preferred_element_type=jnp.float32)
    router = jax.nn.softmax(logits, axis=-1)
    expert_iota = jnp.arange(experts, dtype=jnp.int32)
    route_flat = route_ids.reshape(row_count * 2)
    pair_hits = (route_flat[:, None] == expert_iota).astype(jnp.int32)
    earlier = jnp.cumsum(pair_hits, axis=0, dtype=jnp.int32) - pair_hits
    slot_index = jnp.sum(earlier * pair_hits, axis=1, dtype=jnp.int32)
    target = route_flat * capacity + slot_index
    gate_table = (route_ids.reshape(row_count, 2)[:, :, None] == expert_iota).astype(jnp.float32)
    gate_values = jnp.einsum("rke,re->rk", gate_table, router, precision=lax.Precision.HIGHEST)
    send_rows = (
        jnp.zeros((experts * capacity, D), lowtype).at[target].set(jnp.repeat(hidden2, 2, axis=0))
    )
    send_rows = send_rows.reshape(experts, capacity, D)
    arrived = lax.all_to_all(send_rows, "expert", split_axis=0, concat_axis=0, tiled=True)
    pre_act = (
        jnp.einsum("scd,df->scf", arrived, expert_in[0], preferred_element_type=jnp.float32)
        + expert_in_bias[0]
    )
    activation = jax.nn.gelu(pre_act).astype(lowtype)
    answer = (
        jnp.einsum("scf,fd->scd", activation, expert_out[0], preferred_element_type=jnp.float32)
        + expert_out_bias[0]
    )
    delivered = (answer.astype(lowtype), arrived, pre_act)
    answer_rows = delivered[0]
    arrived = delivered[1]
    returned = lax.all_to_all(answer_rows, "expert", split_axis=0, concat_axis=0, tiled=True)
    picked = (
        returned.reshape(experts * capacity, D)[target].astype(jnp.float32).reshape(row_count, 2, D)
    )
    combined = jnp.sum(gate_values[:, :, None] * picked, axis=1)
    output = (resid + combined).astype(lowtype).reshape(images, length, D)
    upstream = cotangent.astype(jnp.float32).reshape(row_count, D)
    gate_grad = jnp.sum(upstream[:, None, :] * picked, axis=2)
    answer_grad = (
        (gate_values[:, :, None] * upstream[:, None, :]).reshape(row_count * 2, D).astype(lowtype)
    )
    grad_send = (
        jnp.zeros((experts * capacity, D), lowtype)
        .at[target]
        .set(answer_grad)
        .reshape(experts, capacity, D)
    )
    grad_arrived = lax.all_to_all(grad_send, "expert", split_axis=0, concat_axis=0, tiled=True)
    pre_act = delivered[2]
    activation, gelu_back = jax.vjp(jax.nn.gelu, pre_act)
    activation_low = activation.astype(lowtype)
    hidden_grad = jnp.einsum(
        "scd,fd->scf", grad_arrived, expert_out[0], preferred_element_type=jnp.float32
    )
    pre_grad = gelu_back(hidden_grad)[0].astype(lowtype)
    grad_w_out = jnp.einsum(
        "scf,scd->fd", activation_low, grad_arrived, preferred_element_type=jnp.float32
    )
    grad_b_out = jnp.sum(grad_arrived, axis=(0, 1), dtype=jnp.float32)
    grad_w_in = jnp.einsum("scd,scf->df", arrived, pre_grad, preferred_element_type=jnp.float32)
    grad_b_in = jnp.sum(pre_grad, axis=(0, 1), dtype=jnp.float32)
    row_grad = jnp.einsum(
        "scf,df->scd", pre_grad, expert_in[0], preferred_element_type=jnp.float32
    ).astype(lowtype)
    back_rows = lax.all_to_all(row_grad, "expert", split_axis=0, concat_axis=0, tiled=True)
    expert_part = (
        back_rows.reshape(experts * capacity, D)[target]
        .astype(jnp.float32)
        .reshape(row_count, 2, D)
    )
    expert_part = jnp.sum(expert_part, axis=1)
    prob_grad = jnp.einsum("rke,rk->re", gate_table, gate_grad, precision=lax.Precision.HIGHEST)
    logit_grad = router * (prob_grad - jnp.sum(router * prob_grad, axis=-1, keepdims=True))
    logit_grad = logit_grad.astype(lowtype)
    grad_router = jnp.einsum("rd,re->de", hidden2, logit_grad, preferred_element_type=jnp.float32)
    hidden2_grad = expert_part + jnp.einsum(
        "re,de->rd", logit_grad, router_weight, preferred_element_type=jnp.float32
    )
    grad_gain2, grad_shift2, norm2_input = norm_back(hidden2_grad, normed2, inv_dev2, norm2_gain)
    resid_grad = upstream + norm2_input
    attn_grad = resid_grad.astype(lowtype)
    grad_out_w = jnp.einsum("rd,re->de", mixed_rows, attn_grad, preferred_element_type=jnp.float32)
    grad_out_b = jnp.sum(attn_grad, axis=0, dtype=jnp.float32)
    mixed_grad = jnp.einsum("re,de->rd", attn_grad, out_weight, preferred_element_type=jnp.float32)
    mixed_grad = mixed_grad.astype(lowtype).reshape(images, length, HEADS, HEAD)
    scores_again = (
        jnp.einsum("bqhd,bkhd->bhqk", query_rows, key_rows, preferred_element_type=jnp.float32)
        * inv_root
    )
    probs_again = jnp.exp(scores_again - log_total)
    value_grad = jnp.einsum(
        "bhqk,bqhd->bkhd",
        probs_again.astype(lowtype),
        mixed_grad,
        preferred_element_type=jnp.float32,
    )
    weight_grad = jnp.einsum(
        "bqhd,bkhd->bhqk", mixed_grad, value_rows, preferred_element_type=jnp.float32
    )
    score_grad = probs_again * (
        weight_grad - jnp.sum(probs_again * weight_grad, axis=-1, keepdims=True)
    )
    score_grad = score_grad.astype(lowtype)
    query_grad = (
        jnp.einsum("bhqk,bkhd->bqhd", score_grad, key_rows, preferred_element_type=jnp.float32)
        * inv_root
    )
    key_grad = (
        jnp.einsum("bhqk,bqhd->bkhd", score_grad, query_rows, preferred_element_type=jnp.float32)
        * inv_root
    )
    qkv_grad = (
        jnp.stack([query_grad, key_grad, value_grad], axis=2)
        .reshape(row_count, 3 * D)
        .astype(lowtype)
    )
    grad_qkv_w = jnp.einsum("rd,rf->df", hidden1, qkv_grad, preferred_element_type=jnp.float32)
    qkv_sums = jnp.sum(qkv_grad, axis=0, dtype=jnp.float32)
    grad_qv_b = jnp.stack([qkv_sums[:D], qkv_sums[2 * D :]])
    hidden1_grad = jnp.einsum("rf,df->rd", qkv_grad, qkv_weight, preferred_element_type=jnp.float32)
    grad_gain1, grad_shift1, norm1_input = norm_back(hidden1_grad, normed1, inv_dev1, norm1_gain)
    input_grad = (resid_grad + norm1_input).reshape(images, length, D)
    grad_w_in = grad_w_in[None]
    grad_b_in = grad_b_in[None]
    grad_w_out = grad_w_out[None]
    grad_b_out = grad_b_out[None]
    dense_total = lax.psum(
        (
            grad_gain1,
            grad_shift1,
            grad_qkv_w,
            grad_qv_b,
            grad_out_w,
            grad_out_b,
            grad_gain2,
            grad_shift2,
            grad_router,
        ),
        ("dp", "expert"),
    )
    expert_total = (
        lax.psum_scatter(grad_w_in, "dp", scatter_dimension=2, tiled=True),
        lax.psum_scatter(grad_b_in, "dp", scatter_dimension=1, tiled=True),
        lax.psum_scatter(grad_w_out, "dp", scatter_dimension=1, tiled=True),
        lax.psum_scatter(grad_b_out, "dp", scatter_dimension=1, tiled=True),
    )
    return (
        output,
        input_grad,
        dense_total[0],
        dense_total[1],
        dense_total[2],
        dense_total[3],
        dense_total[4],
        dense_total[5],
        dense_total[6],
        dense_total[7],
        dense_total[8],
        expert_total[0],
        expert_total[1],
        expert_total[2],
        expert_total[3],
    )


def solution(mesh):
    return jax.shard_map(
        local,
        mesh=mesh,
        in_specs=(
            P(("dp", "expert"), None, None),
            P(("dp", "expert"), None, None),
            P(("dp", "expert"), None, None),
            P(),
            P(),
            P(),
            P(),
            P(),
            P(),
            P(),
            P(),
            P(),
            P("expert", None, None),
            P("expert", None),
            P("expert", None, None),
            P("expert", None),
        ),
        out_specs=(
            P(("dp", "expert"), None, None),
            P(("dp", "expert"), None, None),
            P(),
            P(),
            P(),
            P(),
            P(),
            P(),
            P(),
            P(),
            P(),
            P("expert", None, "dp"),
            P("expert", "dp"),
            P("expert", "dp", None),
            P("expert", "dp"),
        ),
        check_vma=False,
    )
```

profile of v0, /device:TPU:0, one launch (start us, length us, event | category | flops | bytes accessed | tf_op | source)
XLA Modules:
  0.0 786.5 jit_solution(2210774095803557031)
XLA Ops:
  26.0 4.2 fusion.18
  30.2 6.6 reshape.311
  36.8 5.0 fusion.71
  41.8 2.9 copy.136
  58.0 3.4 convert_element_type.120
  80.8 3.9 reshape.287
  84.7 7.6 scatter_custom_fusion
  92.3 3.2 reshape.253
  95.5 4.9 all-to-all-start
  105.7 3.6 mul.255
  109.3 4.2 mul.256
  122.9 10.9 %scatter_custom_fusion.1 = bf16[1180,768]{1,0:T(8,128)(2,1)} fusion(s32[788]{0:T(1024)S(1)} %copy-done.38, f32[788,768]{1,0:T(8,128)} %mul.256, f32[788]{0:T(1024)S(1)} %mul.253, bf16[]{:T(256)} %constant.15.clone.1), kind=kCustom, calls=%fused_computation.68 | custom fusion | flops 1210368 | bytes 4237314 | tf_op jit(solution)/shard_map/scatter | solution.py:130
  133.8 3.2 reshape.258
  137.0 4.6 all-to-all-start.2
  142.2 11.6 %fusion.13 = f32[4,295,3072]{2,1,0:T(8,128)} fusion(bf16[4,295,768]{2,1,0:T(8,128)(2,1)} %all-to-all-done, bf16[1,768,3072]{2,1,0:T(8,128)(2,1)} %param.28), kind=kOutput, calls=%fused_computation.29 | convolution fusion | flops 5567938560 | bytes 21030912 | tf_op jit(solution)/shard_map/scd,df->scf/dot_general | solution.py:105
  153.9 11.1 %all-to-all-done.2 = bf16[4,295,768]{2,1,0:T(8,128)(2,1)} async-done(((bf16[4,295,768]{2,1,0:T(8,128)(2,1)}), bf16[4,295,768]{2,1,0:T(8,128)(2,1)}, u32[]{:S(2)}, u32[]{:S(2)}) %all-to-all-start.2) | async-done | bytes 1812512 | tf_op jit(solution)/shard_map/all_to_all | solution.py:133
  164.9 19.3 %convert_reduce_fusion = (f32[3072]{0:T(1024)}, bf16[4,295,3072]{2,1,0:T(8,128)(2,1)S(1)}) fusion(f32[4,295,3072]{2,1,0:T(8,128)} %fusion.13, f32[3072]{0:T(1024)} %bitcast.141, bf16[4,295,768]{2,1,0:T(8,128)(2,1)} %all-to-all-done.2, bf16[1,3072,768]{2,1,0:T(8,128)(2,1)} %param.30), kind=kOutput, calls=%fused_computation.13 | convolution fusion | flops 5651309568 | bytes 28305408 | tf_op jit(solution)/shard_map/scd,fd->scf/dot_general | solution.py:137
  184.2 3.0 copy-done.46
  187.3 9.4 %fusion.27 = bf16[4,295,768]{2,1,0:T(8,128)(2,1)} fusion(bf16[4,295,3072]{2,1,0:T(8,128)(2,1)S(1)} %get-tuple-element.117, bf16[1,768,3072]{2,1,0:T(8,128)(2,1)} %param.28), kind=kOutput, calls=%fused_computation.46 | convolution fusion | flops 5568844800 | bytes 13780992 | tf_op jit(solution)/shard_map/scf,df->scd/dot_general | solution.py:147
  196.7 4.6 all-to-all-start.3
  201.3 14.5 %add_convert_fusion = bf16[4,295,768]{2,1,0:T(8,128)(2,1)} fusion(f32[768]{0:T(1024)S(1)} %reduce.11, bf16[1,3072,768]{2,1,0:T(8,128)(2,1)} %param.30, f32[4,295,3072]{2,1,0:T(8,128)} %fusion.13, f32[3072]{0:T(1024)} %bitcast.142), kind=kOutput, calls=%fused_computation.37 | convolution fusion | flops 5606000640 | bytes 21046272 | tf_op jit(solution)/shard_map/scf,fd->scd/dot_general | solution.py:110
  215.9 8.2 %all-to-all-done.3 = bf16[4,295,768]{2,1,0:T(8,128)(2,1)} async-done(((bf16[4,295,768]{2,1,0:T(8,128)(2,1)}), bf16[4,295,768]{2,1,0:T(8,128)(2,1)}, u32[]{:S(2)}, u32[]{:S(2)}) %all-to-all-start.3) | async-done | bytes 1812512 | tf_op jit(solution)/shard_map/all_to_all | solution.py:150
  224.1 4.4 all-to-all-start.1
  242.0 3.2 reshape.259
  245.2 6.9 gather_fusion.1
  252.1 3.8 reshape.266
  255.9 5.6 reduce_sum.227
  261.6 3.2 reshape.254
  264.8 6.5 gather_fusion
  271.2 3.8 reshape.263
  275.1 8.2 %multiply_reduce_fusion.2 = (f32[394,2]{1,0:T(8,128)S(1)}, f32[394,768]{1,0:T(8,128)}) fusion(f32[394,2,768]{2,1,0:T(2,128)} %reshape.263, f32[394,768]{1,0:T(8,128)} %reshape.265, f32[394,2]{1,0:T(8,128)} %bitcast.134), kind=kLoop, calls=%fused_computation.44 | loop fusion | flops 2117356 | bytes 4847776 | tf_op jit(solution)/shard_map/reduce_sum | solution.py:123
  283.2 4.2 fusion.53
  289.4 3.4 multiply_reduce_fusion.4
  297.3 3.0 reshape.312
  303.3 3.8 fusion.30
  307.1 3.9 multiply_reduce_fusion
  315.1 3.9 copy.113
  318.9 6.7 convert_element_type.139
  325.7 7.1 fusion.75
  335.0 11.4 %convolution_bitcast_fusion.1 = f32[1,768,3072]{2,1,0:T(8,128)} fusion(bf16[4,295,768]{2,1,0:T(8,128)(2,1)} %all-to-all-done, bf16[4,295,3072]{2,1,0:T(8,128)(2,1)} %copy-done.46), kind=kOutput, calls=%fused_computation.16 | convolution fusion | flops 5567938560 | bytes 18499584 | tf_op jit(solution)/shard_map/scd,scf->df/dot_general | solution.py:145
  346.5 15.0 %convolution_bitcast_fusion = f32[1,3072,768]{2,1,0:T(8,128)} fusion(bf16[4,295,768]{2,1,0:T(8,128)(2,1)} %all-to-all-done.2, f32[4,295,3072]{2,1,0:T(8,128)} %fusion.13, f32[3072]{0:T(1024)} %bitcast.143), kind=kOutput, calls=%fused_computation.15 | convolution fusion | flops 5604188160 | bytes 25761792 | tf_op jit(solution)/shard_map/scf,scd->fd/dot_general | solution.py:141
  362.9 15.6 %reduce-scatter.13.cloned.1.call-done = f32[384,1]{1,0:T(8,128)} async-done(((f32[3072,1]{1,0:T(8,128)}), f32[384,1]{1,0:T(8,128)}) %reduce-scatter.13.cloned.1.call-update) | async-done | bytes 1552
  384.5 5.4 multiply_reduce_fusion.5
  393.9 3.0 copy.117
  403.4 47.0 %all-reduce.1 = (f32[768]{0:T(1024)}, f32[768]{0:T(1024)}, f32[2,768]{1,0:T(2,128)}, f32[768]{0:T(1024)}, f32[768]{0:T(1024)}, /*index=5*/f32[768]{0:T(1024)}, f32[768,4]{0,1:T(4,128)}) all-reduce(f32[768]{0:T(1024)} %get-tuple-element.77, f32[768]{0:T(1024)} %get-tuple-element.84, ...), channel_id=1, replica_groups=mesh['dp'=8,'expert'=4] {'dp','expert'}, use_global_device_ids=true, to_apply=%region_23.24 | all-reduce | flops 8448 | bytes 67584 | tf_op jit(solution)/shard_map/psum | solution.py:212
  450.4 249.6 %all-reduce.5.cloned.1.call-done = (f32[768,2304]{1,0:T(8,128)}, f32[768,768]{1,0:T(8,128)}) async-done(((f32[768,2304]{1,0:T(8,128)}, f32[768,768]{1,0:T(8,128)}), (f32[768,2304]{1,0:T(8,128)}, f32[768,768]{1,0:T(8,128)})) %all-reduce.5.cloned.1.call-update) | async-done | bytes 9437200 | tf_op jit(solution)/shard_map/psum | solution.py:212
  700.0 71.0 %reduce-scatter.11.cloned.1.call-done = f32[1,384,768]{2,1,0:T(8,128)} async-done(((f32[1,3072,768]{2,1,0:T(8,128)}), f32[1,384,768]{2,1,0:T(8,128)}) %reduce-scatter.11.cloned.1.call-update) | async-done | bytes 1179664 | tf_op jit(solution)/shard_map/reduce_scatter | solution.py:229
  771.0 6.6 copy.148
  (198 shorter events, 114.3 us)
Async XLA Ops:
  8.0 17.9 %copy-start = (bf16[768,2304]{1,0:T(8,128)(2,1)S(1)}, bf16[768,2304]{1,0:T(8,128)(2,1)}, u32[]{:S(2)}) copy-start(bf16[768,2304]{1,0:T(8,128)(2,1)} %param.21) | copy-start | bytes 10616836
  8.0 4.6 copy-start.10
  8.0 8.0 %copy-start.31 = (s32[2,197,2]{1,2,0:T(2,128)S(1)}, s32[2,197,2]{1,2,0:T(2,128)}, u32[]{:S(2)}) copy-start(s32[2,197,2]{1,2,0:T(2,128)} %param.17) | copy-start | bytes 9460
  10.4 15.6 %copy-start.39 = (f32[768]{0:T(1024)S(1)}, f32[768]{0:T(1024)}, u32[]{:S(2)}) copy-start(f32[768]{0:T(1024)} %param.19) | copy-start | bytes 9220
  52.8 2.3 copy-start.1
  52.8 2.2 copy-start.22
  52.8 2.2 copy-start.17
  56.3 5.1 copy-start.45
  64.1 1.3 copy-start.27
  79.1 5.5 copy-start.42
  84.7 7.6 copy-start.37
  95.5 4.9 copy-start.32
  95.5 41.5 %all-to-all-start = ((bf16[4,295,768]{2,1,0:T(8,128)(2,1)}), bf16[4,295,768]{2,1,0:T(8,128)(2,1)}, u32[]{:S(2)}, u32[]{:S(2)}) async-start(bf16[4,295,768]{2,1,0:T(8,128)(2,1)} %reshape.253), calls=%async_computation | async-start | bytes 3637248 | tf_op jit(solution)/shard_map/all_to_all | solution.py:103
  109.3 4.2 copy-start.35
  116.8 6.0 copy-start.38
  137.0 28.0 %all-to-all-start.2 = ((bf16[4,295,768]{2,1,0:T(8,128)(2,1)}), bf16[4,295,768]{2,1,0:T(8,128)(2,1)}, u32[]{:S(2)}, u32[]{:S(2)}) async-start(bf16[4,295,768]{2,1,0:T(8,128)(2,1)} %reshape.258), calls=%async_computation.2 | async-start | bytes 3637248 | tf_op jit(solution)/shard_map/all_to_all | solution.py:133
  184.2 3.0 copy-start.46
  196.7 27.4 %all-to-all-start.3 = ((bf16[4,295,768]{2,1,0:T(8,128)(2,1)}), bf16[4,295,768]{2,1,0:T(8,128)(2,1)}, u32[]{:S(2)}, u32[]{:S(2)}) async-start(bf16[4,295,768]{2,1,0:T(8,128)(2,1)} %fusion.27), calls=%async_computation.3 | async-start | bytes 3637248 | tf_op jit(solution)/shard_map/all_to_all | solution.py:150
  215.9 14.1 %copy-start.40 = (f32[768]{0:T(1024)S(1)}, f32[768]{0:T(1024)}, u32[]{:S(2)}) copy-start(f32[768]{0:T(1024)} %param.19) | copy-start | bytes 9220
  224.1 37.5 %all-to-all-start.1 = ((bf16[4,295,768]{2,1,0:T(8,128)(2,1)}), bf16[4,295,768]{2,1,0:T(8,128)(2,1)}, u32[]{:S(2)}, u32[]{:S(2)}) async-start(bf16[4,295,768]{2,1,0:T(8,128)(2,1)} %add_convert_fusion), calls=%async_computation.1 | async-start | bytes 3637248 | tf_op jit(solution)/shard_map/all_to_all | solution.py:116
  228.5 133.1 %reduce-scatter.15.cloned.1.call-start = ((), (), s32[]{:S(2)}) async-start(), calls=%async_computation.11 | async-start | bytes 442368
  235.5 143.0 %reduce-scatter.13.cloned.1.call-start = ((), (), s32[]{:S(2)}) async-start(), calls=%async_computation.10 | async-start | bytes 1769472
  241.9 458.0 %all-reduce.5.cloned.1.call-start = ((), (), s32[]{:S(2)}) async-start(), calls=%async_computation.12 | async-start | bytes 18874368 | tf_op jit(solution)/shard_map/psum | solution.py:212
  275.1 8.2 %copy-start.23 = (s32[394,2]{1,0:T(8,128)S(1)}, s32[394,2]{1,0:T(8,128)}, u32[]{:S(2)}) copy-start(s32[394,2]{1,0:T(8,128)} %copy.103) | copy-start | bytes 9460
  288.5 4.3 copy-start.3
  288.5 4.3 copy-start.4
  288.5 4.3 copy-start.15
  288.5 4.3 copy-start.28
  288.5 4.3 copy-start.30
  288.5 4.3 copy-start.34
  289.4 3.4 copy-start.36
  292.8 3.0 copy-start.16
  303.3 3.8 copy-start.11
  303.3 3.8 copy-start.18
  303.3 3.8 copy-start.21
  303.3 7.7 slice-start
  307.1 3.9 slice-start.1
  325.7 7.1 copy-start.6
  325.7 7.1 copy-start.13
  335.0 365.0 %reduce-scatter.9.cloned.1.call-start = ((), (), s32[]{:S(2)}) async-start(), calls=%async_computation.8 | async-start | bytes 10616832 | tf_op jit(solution)/shard_map/reduce_scatter | solution.py:227
  346.4 424.6 %reduce-scatter.11.cloned.1.call-start = ((), (), s32[]{:S(2)}) async-start(), calls=%async_computation.9 | async-start | bytes 10616832 | tf_op jit(solution)/shard_map/reduce_scatter | solution.py:229
  384.5 5.4 copy-start.7
  384.5 5.4 copy-start.8
  384.5 5.4 copy-start.41
  384.5 5.4 copy-start.43
  384.5 5.4 copy-start.44
  393.9 3.0 copy-start.26
  771.0 6.6 copy-start.19
  (10 other events, 8.9 us)
Sparse Core Ops, SparseCore 0:
  235.6 63.8 reduce-scatter.14
  303.3 75.1 reduce-scatter.12
  382.7 186.2 reduce-scatter.8
  573.0 197.9 reduce-scatter.10
Sparse Core Ops, SparseCore 1:
  335.0 364.9 all-reduce.4
where the time goes:
time: 797 us; the launch traced here: 787 us
  waiting for transfers between devices  356 us (45%)
  local copies, waits for them, and re-layouts  166 us (21%)
  matrix products  130 us (16%)
  other arithmetic  52.9 us (7%)
  blocking collectives  47 us (6%)
  starting transfers between devices  18.7 us (2%)
  between operations  16.3 us (2%)
    psum x1, waiting for transfers between devices, local(): lax.psum((grad_gain1, grad_shift1, grad_qkv_w, grad_qv_b, grad_out_w, gra...  250 us
    reduce_scatter x1, waiting for transfers between devices, local(): lax.psum_scatter(grad_w_out, 'dp', scatter_dimension=1, tiled=True)  71 us
    psum x1, blocking collectives, local(): lax.psum((grad_gain1, grad_shift1, grad_qkv_w, grad_qv_b, grad_out_w, gra...  47 us
    unnamed x114, local copies, waits for them, and re-layouts  42.8 us
    dot_general x1, matrix products, local(): jnp.einsum('scd,fd->scf', grad_arrived, expert_out[0], preferred_element_...  19.3 us
  transfers between devices with their start and end apart: 9, of which 5 were waited for; matrix products, arithmetic and copies ran while one was open for 28% of the time, Pallas kernels for 0%

commit v1 on v0

--- a/solution.py
+++ b/solution.py
@@ -52,7 +52,7 @@
     length = tokens.shape[1]
     row_count = images * length
     experts = lax.axis_size("expert")
-    capacity = 3 * row_count // experts
+    capacity = -(-(3 * row_count // experts) // 16) * 16
     inv_root = 1.0 / math.sqrt(HEAD)
     lowtype = jnp.bfloat16
     inputs = tokens.astype(jnp.float32).reshape(row_count, D)
@@ -88,19 +88,32 @@
     hidden2 = (normed2 * norm2_gain + norm2_shift).astype(lowtype)
     logits = jnp.dot(hidden2, router_weight, preferred_element_type=jnp.float32)
     router = jax.nn.softmax(logits, axis=-1)
+    route_pairs = route_ids.reshape(row_count, 2)
     expert_iota = jnp.arange(experts, dtype=jnp.int32)
-    route_flat = route_ids.reshape(row_count * 2)
-    pair_hits = (route_flat[:, None] == expert_iota).astype(jnp.int32)
-    earlier = jnp.cumsum(pair_hits, axis=0, dtype=jnp.int32) - pair_hits
-    slot_index = jnp.sum(earlier * pair_hits, axis=1, dtype=jnp.int32)
-    target = route_flat * capacity + slot_index
-    gate_table = (route_ids.reshape(row_count, 2)[:, :, None] == expert_iota).astype(jnp.float32)
-    gate_values = jnp.einsum("rke,re->rk", gate_table, router, precision=lax.Precision.HIGHEST)
-    send_rows = (
-        jnp.zeros((experts * capacity, D), lowtype).at[target].set(jnp.repeat(hidden2, 2, axis=0))
-    )
+    hits = (route_pairs[:, :1] == expert_iota) | (route_pairs[:, 1:] == expert_iota)
+    before = lax.broadcasted_iota(jnp.int32, (row_count, row_count), 0) > (
+        lax.broadcasted_iota(jnp.int32, (row_count, row_count), 1)
+    )
+    slot_index = jnp.dot(
+        before.astype(lowtype), hits.astype(lowtype), preferred_element_type=jnp.float32
+    ).astype(jnp.int32)
+    slot_index = jnp.where(hits, slot_index, -1)
+    slot_iota = jnp.arange(capacity, dtype=jnp.int32)
+    place = slot_index[:, :, None] == slot_iota
+    place_low = place.astype(lowtype).reshape(row_count, experts * capacity)
+    cotangent_rows = cotangent.reshape(row_count, D)
+    upstream = cotangent_rows.astype(jnp.float32)
+    send_rows = jnp.einsum(
+        "rs,rd->sd", place_low, hidden2, preferred_element_type=jnp.float32
+    ).astype(lowtype)
     send_rows = send_rows.reshape(experts, capacity, D)
     arrived = lax.all_to_all(send_rows, "expert", split_axis=0, concat_axis=0, tiled=True)
+    slot_gate = jnp.sum(jnp.where(place, router[:, :, None], 0.0), axis=0).reshape(-1, 1)
+    grad_send = jnp.einsum("rs,rd->sd", place_low, cotangent_rows, preferred_element_type=jnp.float32)
+    grad_send = (grad_send * slot_gate).astype(lowtype).reshape(experts, capacity, D)
+    grad_arrived = lax.all_to_all(grad_send, "expert", split_axis=0, concat_axis=0, tiled=True)
+    place_gate = (place * router[:, :, None]).astype(lowtype)
+    place_gate = place_gate.reshape(row_count, experts * capacity)
     pre_act = (
         jnp.einsum("scd,df->scf", arrived, expert_in[0], preferred_element_type=jnp.float32)
         + expert_in_bias[0]
@@ -114,23 +127,6 @@
     answer_rows = delivered[0]
     arrived = delivered[1]
     returned = lax.all_to_all(answer_rows, "expert", split_axis=0, concat_axis=0, tiled=True)
-    picked = (
-        returned.reshape(experts * capacity, D)[target].astype(jnp.float32).reshape(row_count, 2, D)
-    )
-    combined = jnp.sum(gate_values[:, :, None] * picked, axis=1)
-    output = (resid + combined).astype(lowtype).reshape(images, length, D)
-    upstream = cotangent.astype(jnp.float32).reshape(row_count, D)
-    gate_grad = jnp.sum(upstream[:, None, :] * picked, axis=2)
-    answer_grad = (
-        (gate_values[:, :, None] * upstream[:, None, :]).reshape(row_count * 2, D).astype(lowtype)
-    )
-    grad_send = (
-        jnp.zeros((experts * capacity, D), lowtype)
-        .at[target]
-        .set(answer_grad)
-        .reshape(experts, capacity, D)
-    )
-    grad_arrived = lax.all_to_all(grad_send, "expert", split_axis=0, concat_axis=0, tiled=True)
     pre_act = delivered[2]
     activation, gelu_back = jax.vjp(jax.nn.gelu, pre_act)
     activation_low = activation.astype(lowtype)
@@ -142,19 +138,40 @@
         "scf,scd->fd", activation_low, grad_arrived, preferred_element_type=jnp.float32
     )
     grad_b_out = jnp.sum(grad_arrived, axis=(0, 1), dtype=jnp.float32)
-    grad_w_in = jnp.einsum("scd,scf->df", arrived, pre_grad, preferred_element_type=jnp.float32)
+    grad_w_in = jnp.einsum("scf,scd->fd", pre_grad, arrived, preferred_element_type=jnp.float32)
     grad_b_in = jnp.sum(pre_grad, axis=(0, 1), dtype=jnp.float32)
     row_grad = jnp.einsum(
         "scf,df->scd", pre_grad, expert_in[0], preferred_element_type=jnp.float32
     ).astype(lowtype)
     back_rows = lax.all_to_all(row_grad, "expert", split_axis=0, concat_axis=0, tiled=True)
-    expert_part = (
-        back_rows.reshape(experts * capacity, D)[target]
-        .astype(jnp.float32)
-        .reshape(row_count, 2, D)
-    )
-    expert_part = jnp.sum(expert_part, axis=1)
-    prob_grad = jnp.einsum("rke,rk->re", gate_table, gate_grad, precision=lax.Precision.HIGHEST)
+    parts = lax.axis_size("dp")
+    width = grad_w_out.shape[0] // parts
+    bias_in = grad_b_in.reshape(parts, 1, width)
+    bias_in = jnp.pad(bias_in, ((0, 0), (0, 0), (0, -width % D))).reshape(parts, -1, D)
+    bias_out = grad_b_out.reshape(parts, 1, D // parts)
+    bias_out = jnp.pad(bias_out, ((0, 0), (0, 0), (0, D - D // parts)))
+    bias_rows = jnp.concatenate([bias_in, bias_out], axis=1)
+    bias_rows = jnp.pad(bias_rows, ((0, 0), (0, 16 - bias_rows.shape[1]), (0, 0)))
+    expert_pack = jnp.concatenate(
+        [
+            grad_w_out.astype(lowtype).reshape(parts, width, D),
+            grad_w_in.astype(lowtype).reshape(parts, width, D),
+            bias_rows.astype(lowtype),
+        ],
+        axis=1,
+    )
+    back_rows, returned, expert_pack = lax.optimization_barrier((back_rows, returned, expert_pack))
+    expert_sum = lax.psum_scatter(expert_pack, "dp", scatter_dimension=0, tiled=True)
+    returned = returned.reshape(experts * capacity, D)
+    combined = jnp.dot(place_gate, returned, preferred_element_type=jnp.float32)
+    output = (resid + combined).astype(lowtype).reshape(images, length, D)
+    expert_part = jnp.dot(
+        place_low, back_rows.reshape(experts * capacity, D), preferred_element_type=jnp.float32
+    )
+    pair_grad = jnp.einsum(
+        "rd,sd->rs", cotangent_rows, returned, preferred_element_type=jnp.float32
+    ).reshape(row_count, experts, capacity)
+    prob_grad = jnp.sum(jnp.where(place, pair_grad, 0.0), axis=-1)
     logit_grad = router * (prob_grad - jnp.sum(router * prob_grad, axis=-1, keepdims=True))
     logit_grad = logit_grad.astype(lowtype)
     grad_router = jnp.einsum("rd,re->de", hidden2, logit_grad, preferred_element_type=jnp.float32)
@@ -205,46 +222,48 @@
     hidden1_grad = jnp.einsum("rf,df->rd", qkv_grad, qkv_weight, preferred_element_type=jnp.float32)
     grad_gain1, grad_shift1, norm1_input = norm_back(hidden1_grad, normed1, inv_dev1, norm1_gain)
     input_grad = (resid_grad + norm1_input).reshape(images, length, D)
-    grad_w_in = grad_w_in[None]
-    grad_b_in = grad_b_in[None]
-    grad_w_out = grad_w_out[None]
-    grad_b_out = grad_b_out[None]
-    dense_total = lax.psum(
-        (
-            grad_gain1,
-            grad_shift1,
-            grad_qkv_w,
+    small = jnp.concatenate(
+        [
+            grad_gain1[None],
+            grad_shift1[None],
             grad_qv_b,
-            grad_out_w,
-            grad_out_b,
-            grad_gain2,
-            grad_shift2,
-            grad_router,
-        ),
-        ("dp", "expert"),
-    )
-    expert_total = (
-        lax.psum_scatter(grad_w_in, "dp", scatter_dimension=2, tiled=True),
-        lax.psum_scatter(grad_b_in, "dp", scatter_dimension=1, tiled=True),
-        lax.psum_scatter(grad_w_out, "dp", scatter_dimension=1, tiled=True),
-        lax.psum_scatter(grad_b_out, "dp", scatter_dimension=1, tiled=True),
-    )
+            grad_out_b[None],
+            grad_gain2[None],
+            grad_shift2[None],
+            grad_router.T,
+        ]
+    )
+    small_count = small.shape[0]
+    small = jnp.pad(small, ((0, 128 - small_count), (0, 0))).T
+    dense_pack = jnp.concatenate(
+        [grad_qkv_w.astype(lowtype), grad_out_w.astype(lowtype), small.astype(lowtype)], axis=1
+    )
+    dense_total = lax.psum(dense_pack, ("dp", "expert"))
+    dense_total = dense_total.astype(jnp.float32)
+    small = dense_total[:, 4 * D : 4 * D + small_count].T
+    expert_sum = expert_sum.astype(jnp.float32)[0]
+    total_in = expert_sum[width : 2 * width].T[None]
+    total_out = expert_sum[:width][None]
+    bias_sum = expert_sum[2 * width :]
+    in_rows = -(-width // D)
+    total_b_in = bias_sum[:in_rows].reshape(1, -1)[:, :width]
+    total_b_out = bias_sum[in_rows : in_rows + 1, : D // parts]
     return (
         output,
         input_grad,
-        dense_total[0],
-        dense_total[1],
-        dense_total[2],
-        dense_total[3],
-        dense_total[4],
-        dense_total[5],
-        dense_total[6],
-        dense_total[7],
-        dense_total[8],
-        expert_total[0],
-        expert_total[1],
-        expert_total[2],
-        expert_total[3],
+        small[0],
+        small[1],
+        dense_total[:, : 3 * D],
+        small[2:4],
+        dense_total[:, 3 * D : 4 * D],
+        small[4],
+        small[5],
+        small[6],
+        small[7:].T,
+        total_in,
+        total_b_in,
+        total_out,
+        total_b_out,
     )
 
 

time: 797 us -> 643 us (0.81)
  waiting for transfers between devices: 356 us -> 256 us
  blocking collectives: 47 us -> 0 us
  local copies, waits for them, and re-layouts: 166 us -> 153 us
    reduce_scatter x2 -> x1, waiting for transfers between devices: 71 us -> 0.01 us  [local(): lax.psum_scatter(expert_pack, 'dp', scatter_dimension=0, tiled=True)]
    psum x1 -> x0, blocking collectives: 47 us -> none  [local(): lax.psum((grad_gain1, grad_shift1, grad_qkv_w, grad_qv_b, grad_out_w, gra...]
    unnamed x7 -> x2, waiting for transfers between devices: 15.7 us -> 0.54 us
    slice x1 -> x11, local copies, waits for them, and re-layouts: 0.8 us -> 15 us  [the longest x1 5.48 us: local(): dense_total[:, :3 * D]]
    gather x2 -> x0, local copies, waits for them, and re-layouts: 13.4 us -> none  [the longest x1 6.89 us: local(): back_rows.reshape(experts * capacity, D)[target].astype(jnp.float32)]
    concatenate x0 -> x3, other arithmetic: none -> 13.2 us  [the longest x1 9.52 us: local(): jnp.concatenate([grad_w_out.astype(lowtype).reshape(parts, width, D), gra...]
    dot_general x3 -> x7, matrix products: 18.2 us -> 31 us  [the longest x1 10.6 us: local(): jnp.einsum('scf,scd->fd', pre_grad, arrived, preferred_element_type=jnp.f...]
    scatter x1 -> x0, other arithmetic: 10.9 us -> none  [local(): grad_send = jnp.zeros((experts * capacity, D), lowtype).at[target].set(an...]
  transfers between devices with their start and end apart: 9 -> 6, of which waited for: 5 -> 3; matrix products, arithmetic and copies ran while one was open for 28% -> 23% of each run, Pallas kernels for 0% -> 0%
where the time goes in v1:
time: 643 us; the launch traced here: 631 us
  waiting for transfers between devices  256 us (40%)
  local copies, waits for them, and re-layouts  153 us (24%)
  matrix products  135 us (21%)
  other arithmetic  52.6 us (8%)
  starting transfers between devices  17.9 us (3%)
  between operations  16.6 us (3%)
    psum x1, waiting for transfers between devices, local(): dense_total = lax.psum(dense_pack, ('dp', 'expert'))  244 us
    unnamed x122, local copies, waits for them, and re-layouts  39.3 us
    dot_general x1, matrix products, local(): jnp.einsum('scd,fd->scf', grad_arrived, expert_out[0], preferred_element_...  19.8 us
    dot_general x1, matrix products, local(): jnp.einsum('scd,df->scf', arrived, expert_in[0], preferred_element_type=j...  15.4 us
  transfers between devices with their start and end apart: 6, of which 3 were waited for; matrix products, arithmetic and copies ran while one was open for 23% of the time, Pallas kernels for 0%

profile of v1, /device:TPU:0, one launch (start us, length us, event | category | flops | bytes accessed | tf_op | source)
XLA Modules:
  0.0 631.0 jit_solution(16386979559876044164)
XLA Ops:
  24.5 4.2 fusion.20
  28.8 6.6 %reshape.259 = bf16[2,197,3,12,64]{4,3,2,1,0:T(8,128)(2,1)} reshape(bf16[394,2304]{1,0:T(8,128)(2,1)} %fusion.20) | data formatting | bytes 3631104 | tf_op jit(solution)/shard_map/reshape | solution.py:65
  35.4 5.0 fusion.76
  40.4 2.9 copy.216
  43.3 2.9 copy.215
  46.2 2.9 copy.214
  56.6 3.3 convert_element_type.143
  66.5 2.7 eq.71
  69.2 3.6 eq.75
  76.4 4.3 convolution_convert_fusion.1
  80.7 4.4 all-to-all-start.1
  87.6 3.1 eq.74
  109.0 3.7 fusion.21
  112.8 4.6 all-to-all-start
  117.4 15.4 %multiply_convert_fusion = (bf16[4,304,3072]{2,1,0:T(8,128)(2,1)}, f32[4,304,3072]{2,1,0:T(8,128)}) fusion(f32[3072]{0:T(1024)} %bitcast.141, bf16[4,304,768]{2,1,0:T(8,128)(2,1)} %all-to-all-done.1, bf16[1,768,3072]{2,1,0:T(8,128)(2,1)} %param.28), kind=kOutput, calls=%fused_computation.11 | convolution fusion | flops 5775163392 | bytes 29011968 | tf_op jit(solution)/shard_map/scd,df->scf/dot_general | solution.py:118
  132.7 8.6 %all-to-all-done = bf16[4,304,768]{2,1,0:T(8,128)(2,1)} async-done(((bf16[4,304,768]{2,1,0:T(8,128)(2,1)}), bf16[4,304,768]{2,1,0:T(8,128)(2,1)}, u32[]{:S(2)}, u32[]{:S(2)}) %all-to-all-start) | async-done | bytes 1867808 | tf_op jit(solution)/shard_map/all_to_all | solution.py:114
  141.3 19.8 %fusion.81 = (bf16[3072]{0:T(1024)(128)(2,1)}, bf16[4,304,3072]{2,1,0:T(8,128)(2,1)S(1)}) fusion(f32[4,304,3072]{2,1,0:T(8,128)} %get-tuple-element.129, f32[3072]{0:T(1024)} %bitcast.142, bf16[4,304,768]{2,1,0:T(8,128)(2,1)} %all-to-all-done, bf16[1,3072,768]{2,1,0:T(8,128)(2,1)} %param.30), kind=kOutput, calls=%fused_computation.150 | convolution fusion | flops 5819986944 | bytes 29018112 | tf_op jit(solution)/shard_map/scd,fd->scf/dot_general | solution.py:133
  161.1 3.0 copy-done.51
  164.1 9.9 %fusion.33 = bf16[4,304,768]{2,1,0:T(8,128)(2,1)} fusion(bf16[4,304,3072]{2,1,0:T(8,128)(2,1)S(1)} %get-tuple-element.131, bf16[1,768,3072]{2,1,0:T(8,128)(2,1)} %param.28), kind=kOutput, calls=%fused_computation.52 | convolution fusion | flops 5738741760 | bytes 14057472 | tf_op jit(solution)/shard_map/scf,df->scd/dot_general | solution.py:143
  174.0 4.4 all-to-all-start.2
  178.4 10.6 %bitcast_convert_fusion = bf16[3072,768]{1,0:T(8,128)(2,1)} fusion(bf16[4,304,3072]{2,1,0:T(8,128)(2,1)} %copy-done.51, bf16[4,304,768]{2,1,0:T(8,128)(2,1)} %all-to-all-done.1), kind=kOutput, calls=%fused_computation.13 | convolution fusion | flops 5740167168 | bytes 14057472 | tf_op jit(solution)/shard_map/scf,scd->fd/dot_general | solution.py:141
  189.0 10.5 %add_convert_fusion = bf16[4,304,768]{2,1,0:T(8,128)(2,1)} fusion(f32[768]{0:T(1024)S(1)} %copy-done.49, bf16[4,304,3072]{2,1,0:T(8,128)(2,1)} %get-tuple-element.128, bf16[1,3072,768]{2,1,0:T(8,128)(2,1)} %param.30), kind=kOutput, calls=%fused_computation.36 | convolution fusion | flops 5739675648 | bytes 14060544 | tf_op jit(solution)/shard_map/scf,fd->scd/dot_general | solution.py:123
  201.7 4.4 all-to-all-start.3
  206.2 10.8 %bitcast_convert_fusion.1 = bf16[3072,768]{1,0:T(8,128)(2,1)} fusion(bf16[4,304,3072]{2,1,0:T(8,128)(2,1)} %get-tuple-element.128, bf16[4,304,768]{2,1,0:T(8,128)(2,1)} %all-to-all-done), kind=kOutput, calls=%fused_computation.14 | convolution fusion | flops 5740167168 | bytes 14057472 | tf_op jit(solution)/shard_map/scf,scd->fd/dot_general | solution.py:137
  223.8 6.7 %copy.182 = bf16[8,384,768]{1,2,0:T(8,128)(2,1)} copy(bf16[8,384,768]{2,1,0:T(8,128)(2,1)} %bitcast.135) | data formatting | bytes 9437184 | tf_op jit(solution)/shard_map/reshape | solution.py:158
  230.5 6.7 %copy.181 = bf16[8,384,768]{1,2,0:T(8,128)(2,1)} copy(bf16[8,384,768]{2,1,0:T(8,128)(2,1)} %bitcast.136) | data formatting | bytes 9437184 | tf_op jit(solution)/shard_map/reshape | solution.py:157
  237.2 9.5 %fusion.8 = bf16[8,784,768]{1,2,0:T(8,128)(2,1)} fusion(bf16[8,2,768]{1,2,0:T(8,128)(2,1)} %copy.217, bf16[8,384,768]{1,2,0:T(8,128)(2,1)} %copy.182, bf16[8,384,768]{1,2,0:T(8,128)(2,1)} %copy.181), kind=kLoop, calls=%fused_computation.12 | loop fusion | flops 38535168 | bytes 19095552 | tf_op jit(solution)/shard_map/concatenate | solution.py:155
  246.7 4.0 fusion.39
  250.7 3.8 convolution_bitcast_fusion
  254.5 4.0 reshape.250
  258.4 4.2 select_reduce_fusion.1
  265.2 3.1 multiply_reduce_fusion.2
  272.1 3.0 reshape.260
  275.2 3.1 copy.189
  278.4 3.8 fusion.36
  282.2 3.8 multiply_reduce_fusion
  292.6 3.9 copy.194
  296.5 6.8 %convert_element_type.165 = bf16[394,2304]{0,1:T(8,128)(2,1)} reshape(bf16[2,197,3,12,64]{1,0,4,3,2:T(2,128)(2,1)} %copy.194) | data formatting | bytes 3631104 | tf_op jit(solution)/shard_map/convert_element_type | solution.py:217
  303.3 5.9 multiply_reduce_fusion.3
  314.4 2.8 concatenate.20
  319.7 4.1 convolution_convert_fusion
  329.5 3.7 fusion.45
  338.4 4.0 multiply_add_fusion
  344.9 2.9 copy.200
  347.8 244.4 %all-reduce.6.cloned.1.call-done = bf16[768,3200]{1,0:T(8,128)(2,1)} async-done(((bf16[768,3200]{1,0:T(8,128)(2,1)}), bf16[768,3200]{1,0:T(8,128)(2,1)}) %all-reduce.6.cloned.1.call-update) | async-done | bytes 4915216 | tf_op jit(solution)/shard_map/psum | solution.py:241
  592.2 3.0 convert_element_type.173
  602.3 5.5 slice.128
  607.8 2.9 slice.130
  (208 shorter events, 116.9 us)
Async XLA Ops:
  8.0 16.5 %copy-start = (bf16[768,2304]{1,0:T(8,128)(2,1)S(1)}, bf16[768,2304]{1,0:T(8,128)(2,1)}, u32[]{:S(2)}) copy-start(bf16[768,2304]{1,0:T(8,128)(2,1)} %param.21) | copy-start | bytes 10616836
  8.0 4.6 copy-start.8
  10.4 14.2 %copy-start.39 = (f32[768]{0:T(1024)S(1)}, f32[768]{0:T(1024)}, u32[]{:S(2)}) copy-start(f32[768]{0:T(1024)} %param.19) | copy-start | bytes 9220
  23.2 5.6 copy-start.42
  51.4 2.3 copy-start.1
  51.4 2.2 copy-start.24
  51.4 2.2 copy-start.17
  53.7 1.2 copy-start.25
  54.9 5.1 copy-start.46
  59.9 4.1 copy-start.48
  62.6 12.1 %copy-start.28 = (f32[394]{0:T(512)}, f32[394]{0:T(512)S(1)}, u32[]{:S(2)}) copy-start(f32[394]{0:T(512)S(1)} %broadcast_multiply_fusion.5) | copy-start | bytes 4732
  64.0 10.7 %copy-start.34 = (f32[394]{0:T(512)}, f32[394]{0:T(512)S(1)}, u32[]{:S(2)}) copy-start(f32[394]{0:T(512)S(1)} %add_rsqrt_fusion.1) | copy-start | bytes 4732
  69.2 5.6 copy-start.32
  69.2 5.6 copy-start.47
  76.3 4.4 copy-start.12
  80.7 32.1 %all-to-all-start.1 = ((bf16[4,304,768]{2,1,0:T(8,128)(2,1)}), bf16[4,304,768]{2,1,0:T(8,128)(2,1)}, u32[]{:S(2)}, u32[]{:S(2)}) async-start(bf16[4,304,768]{2,1,0:T(8,128)(2,1)} %bitcast.137), calls=%async_computation.1 | async-start | bytes 3735552 | tf_op jit(solution)/shard_map/all_to_all | solution.py:110
  85.1 9.5 %copy-start.36 = (bf16[768,4]{0,1:T(4,128)(2,1)S(1)}, bf16[768,4]{0,1:T(4,128)(2,1)}, u32[]{:S(2)}) copy-start(bf16[768,4]{0,1:T(4,128)(2,1)} %param.27) | copy-start | bytes 18436
  101.3 7.8 %copy-start.45 = (f32[1216]{0:T(1024)S(1)}, f32[1216]{0:T(1024)}, u32[]{:S(2)}) copy-start(f32[1216]{0:T(1024)} %mul.208) | copy-start | bytes 14596
  112.8 28.6 %all-to-all-start = ((bf16[4,304,768]{2,1,0:T(8,128)(2,1)}), bf16[4,304,768]{2,1,0:T(8,128)(2,1)}, u32[]{:S(2)}, u32[]{:S(2)}) async-start(bf16[4,304,768]{2,1,0:T(8,128)(2,1)} %bitcast.138), calls=%async_computation | async-start | bytes 3735552 | tf_op jit(solution)/shard_map/all_to_all | solution.py:114
  161.1 3.0 copy-start.51
  174.0 27.7 %all-to-all-start.2 = ((bf16[4,304,768]{2,1,0:T(8,128)(2,1)}), bf16[4,304,768]{2,1,0:T(8,128)(2,1)}, u32[]{:S(2)}, u32[]{:S(2)}) async-start(bf16[4,304,768]{2,1,0:T(8,128)(2,1)} %fusion.33), calls=%async_computation.2 | async-start | bytes 3735552 | tf_op jit(solution)/shard_map/all_to_all | solution.py:146
  178.4 10.6 %copy-start.49 = (f32[768]{0:T(1024)S(1)}, f32[768]{0:T(1024)}, u32[]{:S(2)}) copy-start(f32[768]{0:T(1024)} %reduce.9) | copy-start | bytes 9220
  201.7 45.0 %all-to-all-start.3 = ((bf16[4,304,768]{2,1,0:T(8,128)(2,1)}), bf16[4,304,768]{2,1,0:T(8,128)(2,1)}, u32[]{:S(2)}, u32[]{:S(2)}) async-start(bf16[4,304,768]{2,1,0:T(8,128)(2,1)} %add_convert_fusion), calls=%async_computation.3 | async-start | bytes 3735552 | tf_op jit(solution)/shard_map/all_to_all | solution.py:129
  206.1 386.1 %all-reduce.6.cloned.1.call-start = ((), (), s32[]{:S(2)}) async-start(), calls=%async_computation.5 | async-start | bytes 9830400 | tf_op jit(solution)/shard_map/psum | solution.py:241
  246.7 4.0 copy-start.19
  263.7 4.6 copy-start.3
  263.7 4.6 copy-start.20
  263.7 4.6 copy-start.29
  263.7 4.6 copy-start.33
  263.7 4.6 copy-start.35
  268.3 2.2 copy-start.15
  278.3 3.8 copy-start.9
  278.3 3.8 copy-start.18
  278.3 3.8 copy-start.23
  278.4 7.7 %slice-start = ((s8[4915200]{0:T(1024)(128)(4,1)}), s8[4194304]{0:T(1024)(128)(4,1)S(1)}, s32[]{:S(2)}) async-start(s8[4915200]{0:T(1024)(128)(4,1)} %bitcast.133), calls=%async_computation.7 | async-start | bytes 8388608
  282.2 3.9 slice-start.1
  286.0 1.1 copy-start.11
  288.3 1.9 copy-start.7
  288.4 1.9 copy-start.16
  296.5 6.8 %copy-start.40 = (f32[768]{0:T(1024)S(1)}, f32[768]{0:T(1024)}, u32[]{:S(2)}) copy-start(f32[768]{0:T(1024)} %param.19) | copy-start | bytes 9220
  319.7 4.1 copy-start.22
  326.3 286.0 %reduce-scatter.2.cloned.1.call-start = ((), (), s32[]{:S(2)}) async-start(), calls=%async_computation.6 | async-start | bytes 12386304 | tf_op jit(solution)/shard_map/reduce_scatter | solution.py:164
  333.2 5.2 copy-start.50
  333.2 5.2 copy-start.41
  333.2 5.2 copy-start.43
  333.2 5.2 copy-start.44
  607.8 2.9 copy-start.5
  613.8 2.7 copy-start.14
  (12 other events, 10.8 us)
Sparse Core Ops, SparseCore 0:
  326.4 265.7 all-reduce.5
Sparse Core Ops, SparseCore 1:
  330.4 207.6 reduce-scatter.1
